TPU v7x, 32 devices: a whole 2x2x4 slice. The times are simulated.
32 devices in a mesh: dp: 8 (over z, y), seq: 4 (over x, core).
Axes of the slice: x: 2, y: 2, z: 4, core: 2. Of those that a mesh axis runs over, the one named last changes fastest.
Arguments:
- hidden: bfloat16 [8, 512, 4096], P('dp', 'seq'), may hold values from -6 to 6
- query_states: bfloat16 [8, 512, 4096], P('dp', 'seq'), may hold values from -8 to 8
- saved_key_states: bfloat16 [8, 512, 256], P('dp', 'seq'), may hold values from -8 to 8
- saved_value_states: bfloat16 [8, 512, 256], P('dp', 'seq'), may hold values from -6 to 6
- out_grad: bfloat16 [8, 512, 4096], P('dp', 'seq'), may hold values from -6 to 6
- seg_lengths: int32 [8, 8], P('dp'), may hold values from 1 to 256, 512 in all within a row
- weights: float32 [4096, 512], P(('dp', 'seq')), may hold values from -4 to 4
Outputs:
- query_grad: bfloat16 [8, 512, 4096], P('dp', 'seq')
- updated: bfloat16 [4096, 512], P('dp')
Inputs may be any that keep to these rules, and one draw needn't show every extreme that they name: `seg_lengths`: each trajectory's 8 lengths sum to 512; in every trajectory the longest document has exactly 256 tokens.
All inputs are finite; a program needn't handle non-finite values.
Results may differ from a plain program's by a relative error of at most 0.0072.
Values may be sent and summed in bfloat16 or wider, within the bound.
A program may use at most 128 MiB of HBM per device.

v0:
```python
import jax
import jax.numpy as jnp
from jax import lax
from jax.sharding import PartitionSpec as P

KEY_VALUE_HEADS = 2
HEAD_SIZE = 128


learn_rate = 0.5
decay_rate = 0.1


def group_grads(query_heads, key_head, value_head, grad_heads, documents):
    seq_len = query_heads.shape[1]
    head_size = query_heads.shape[2]
    block_rows = min(512, seq_len)
    score_scale = head_size ** (-0.5)
    positions = jnp.arange(seq_len, dtype=jnp.int32)
    key_grad = jnp.zeros((seq_len, head_size), jnp.float32)
    value_grad = jnp.zeros((seq_len, head_size), jnp.float32)
    query_parts = []
    for block_index in range(seq_len // block_rows):
        first_row = block_index * block_rows
        last_row = first_row + block_rows
        query_block = query_heads[:, first_row:last_row]
        grad_block = grad_heads[:, first_row:last_row]
        key_rows = key_head[:last_row]
        value_rows = value_head[:last_row]
        query_pos = positions[first_row:last_row]
        allowed = (positions[None, :last_row] <= query_pos[:, None]) & (
            documents[None, :last_row] == documents[first_row:last_row, None]
        )
        scores = (
            jnp.einsum("hqd,kd->hqk", query_block, key_rows, preferred_element_type=jnp.float32)
            * score_scale
        )
        scores = jnp.where(allowed[None], scores, -1e30)
        shifted = jnp.exp(scores - jnp.max(scores, axis=2, keepdims=True))
        attend = shifted / jnp.sum(shifted, axis=2, keepdims=True)
        prob_grad = jnp.einsum(
            "hqd,kd->hqk", grad_block, value_rows, preferred_element_type=jnp.float32
        )
        row_delta = jnp.sum(attend * prob_grad, axis=2, keepdims=True)
        score_grad = (attend * (prob_grad - row_delta)).astype(jnp.bfloat16)
        query_parts.append(
            (
                jnp.einsum("hqk,kd->hqd", score_grad, key_rows, preferred_element_type=jnp.float32)
                * score_scale
            ).astype(jnp.bfloat16)
        )
        key_grad = key_grad.at[:last_row].add(
            jnp.einsum("hqk,hqd->kd", score_grad, query_block, preferred_element_type=jnp.float32)
            * score_scale
        )
        value_grad = value_grad.at[:last_row].add(
            jnp.einsum(
                "hqk,hqd->kd",
                attend.astype(jnp.bfloat16),
                grad_block,
                preferred_element_type=jnp.float32,
            )
        )
    return (jnp.concatenate(query_parts, axis=1), key_grad, value_grad)


def body(
    hidden, query_states, saved_key_states, saved_value_states, out_grad, seg_lengths, weights
):
    sequence_count = lax.axis_size("seq")
    seq_index = lax.axis_index("seq")
    token_rows = hidden.shape[1]
    seq_len = token_rows * sequence_count
    local_heads = query_states.shape[2] // (HEAD_SIZE * sequence_count)
    query_group_size = sequence_count // KEY_VALUE_HEADS
    query_send = query_states[0].reshape(token_rows, sequence_count, local_heads * HEAD_SIZE)
    grad_send = out_grad[0].reshape(token_rows, sequence_count, local_heads * HEAD_SIZE)
    query_recv, grad_recv = (
        lax.all_to_all(query_send, "seq", split_axis=1, concat_axis=0, tiled=True),
        lax.all_to_all(grad_send, "seq", split_axis=1, concat_axis=0, tiled=True),
    )
    query_heads = query_recv.reshape(seq_len, local_heads, HEAD_SIZE).transpose(1, 0, 2)
    grad_heads = grad_recv.reshape(seq_len, local_heads, HEAD_SIZE).transpose(1, 0, 2)
    pairs = jnp.concatenate(
        [
            saved_key_states[0].reshape(token_rows, KEY_VALUE_HEADS, HEAD_SIZE),
            saved_value_states[0].reshape(token_rows, KEY_VALUE_HEADS, HEAD_SIZE),
        ],
        axis=2,
    )
    key_value_head = seq_index // query_group_size
    all_pairs = lax.all_gather(pairs, "seq", axis=0, tiled=True)
    own_pair = lax.dynamic_index_in_dim(all_pairs, key_value_head, 1, keepdims=False)
    key_head = own_pair[:, :HEAD_SIZE]
    value_head = own_pair[:, HEAD_SIZE:]
    doc_ends = jnp.cumsum(seg_lengths[0])
    positions = jnp.arange(seq_len, dtype=jnp.int32)
    documents = jnp.sum((positions[:, None] >= doc_ends[None, :]).astype(jnp.int32), axis=1)
    query_out, key_total, value_total = group_grads(
        query_heads, key_head, value_head, grad_heads, documents
    )
    query_local = query_out.transpose(1, 0, 2).reshape(seq_len, local_heads * HEAD_SIZE)
    query_grad = lax.all_to_all(query_local, "seq", split_axis=0, concat_axis=1, tiled=True)
    head_pair = jnp.concatenate([key_total, value_total], axis=1)
    head_selector = (jnp.arange(KEY_VALUE_HEADS, dtype=jnp.int32) == key_value_head).astype(
        jnp.float32
    )
    placed = head_pair[:, None, :] * head_selector[None, :, None]
    summed_gradient = lax.psum_scatter(placed, "seq", scatter_dimension=0, tiled=True)
    pair_grad = jnp.concatenate(
        [
            summed_gradient[:, :, :HEAD_SIZE].reshape(token_rows, KEY_VALUE_HEADS * HEAD_SIZE),
            summed_gradient[:, :, HEAD_SIZE:].reshape(token_rows, KEY_VALUE_HEADS * HEAD_SIZE),
        ],
        axis=1,
    ).astype(jnp.bfloat16)
    hidden_rows = hidden[0]
    dp_count = lax.axis_size("dp")
    row_part = weights.shape[0]
    spread = hidden_rows.reshape(token_rows, dp_count, sequence_count, row_part)
    regrouped = lax.all_to_all(spread, "seq", split_axis=2, concat_axis=0, tiled=True).reshape(
        seq_len, dp_count * row_part
    )
    pair_all = lax.all_gather(pair_grad, "seq", axis=0, tiled=True)
    weight_grad = lax.psum_scatter(
        jnp.einsum("td,tc->dc", regrouped, pair_all, preferred_element_type=jnp.float32),
        "dp",
        scatter_dimension=0,
        tiled=True,
    )
    row_norm = jnp.sqrt(jnp.mean(weight_grad * weight_grad, axis=1, keepdims=True) + 1e-06)
    fresh_rows = (
        weights * (1.0 - learn_rate * decay_rate) - learn_rate * weight_grad / row_norm
    ).astype(jnp.bfloat16)
    gathered = lax.all_gather(fresh_rows, "seq", axis=0, tiled=True)
    return (query_grad[None], gathered)


def solution(mesh):
    placed = (
        P("dp", "seq", None),
        P("dp", "seq", None),
        P("dp", "seq", None),
        P("dp", "seq", None),
        P("dp", "seq", None),
        P("dp", None),
        P(("dp", "seq"), None),
    )
    return jax.shard_map(
        body,
        mesh=mesh,
        in_specs=placed,
        out_specs=(P("dp", "seq", None), P("dp", None)),
        check_vma=False,
    )
```

profile of v0, /device:TPU:0, one launch (start us, length us, event | category | flops | bytes accessed | tf_op | source)
XLA Modules:
  0.0 202.5 jit_solution(10850494738340130421)
XLA Ops:
  7.2 0.0 copy-start.6
  7.2 1.9 reshape_squeeze.17
  9.1 1.3 copy.73
  10.4 4.2 %all-to-all-start = ((bf16[128,4,1024]{2,0,1:T(8,128)(2,1)}), bf16[128,4,1024]{2,0,1:T(8,128)(2,1)S(1)}, u32[]{:S(2)}, u32[]{:S(2)}) async-start(bf16[128,4,1024]{2,0,1:T(8,128)(2,1)} %copy.73), calls=%async_computation | async-start | bytes 2097152 | tf_op jit(solution)/shard_map/all_to_all | solution.py:79
  14.6 1.8 reshape_squeeze.18
  16.5 1.3 copy.75
  17.8 11.3 %all-to-all-done = bf16[128,4,1024]{2,0,1:T(8,128)(2,1)S(1)} async-done(((bf16[128,4,1024]{2,0,1:T(8,128)(2,1)}), bf16[128,4,1024]{2,0,1:T(8,128)(2,1)S(1)}, u32[]{:S(2)}, u32[]{:S(2)}) %all-to-all-start) | async-done | bytes 1048608 | tf_op jit(solution)/shard_map/all_to_all | solution.py:79
  29.1 3.5 %all-to-all-start.1 = ((bf16[128,4,1024]{2,0,1:T(8,128)(2,1)}), bf16[128,4,1024]{2,0,1:T(8,128)(2,1)S(1)}, u32[]{:S(2)}, u32[]{:S(2)}) async-start(bf16[128,4,1024]{2,0,1:T(8,128)(2,1)} %copy.75), calls=%async_computation.1 | async-start | bytes 2097152 | tf_op jit(solution)/shard_map/all_to_all | solution.py:80
  32.7 0.2 reduce-window.8
  32.9 1.8 reshape_squeeze.19
  34.7 1.1 copy.86
  35.8 0.6 dynamic-slice.10
  37.1 0.1 convert_reduce_fusion
  37.2 13.5 %all_gather.9 = bf16[512,2,256]{2,0,1:T(8,128)(2,1)S(1)} all-gather(bf16[128,2,256]{2,0,1:T(8,128)(2,1)S(1)} %pad_maximum_fusion.1), channel_id=1, replica_groups=mesh['dp'=8,'seq'=4] {'seq'}, dimensions={0}, use_global_device_ids=true | all-gather | bytes 655360 | tf_op jit(solution)/shard_map/all_gather | solution.py:92
  50.7 0.9 fusion.25
  51.6 0.3 copy.98
  51.9 3.5 %all-to-all-start.3 = ((bf16[128,8,4,128]{3,1,0,2:T(8,128)(2,1)}), bf16[128,8,4,128]{3,1,0,2:T(8,128)(2,1)S(1)}, u32[]{:S(2)}, u32[]{:S(2)}) async-start(bf16[128,8,4,128]{3,1,0,2:T(8,128)(2,1)} %copy.86), calls=%async_computation.3 | async-start | bytes 2097152 | tf_op jit(solution)/shard_map/all_to_all | solution.py:121
  55.5 0.2 reduce-scatter.2.cloned.1.call-start
  55.7 0.0 copy-start.2
  55.7 0.3 copy.99
  56.0 4.5 %fusion.21 = f32[512,8,512]{2,0,1:T(8,128)} fusion(bf16[512,8,128]{2,1,0:T(8,128)(2,1)S(1)} %bitcast.92, bf16[512,256]{1,0:T(8,128)(2,1)S(1)} %dynamic-slice_bitcast_fusion), kind=kOutput, calls=%fused_computation.27 | convolution fusion | flops 536870912 | bytes 9568256 | tf_op jit(solution)/shard_map/hqd,kd->hqk/dot_general | solution.py:35
  60.5 9.3 %fusion.29 = (f32[8,512]{1,0:T(8,128)S(1)}, f32[8,512,512]{1,2,0:T(8,128)S(1)}) fusion(f32[512,8,512]{2,0,1:T(8,128)} %fusion.21, pred[512,512]{0,1:T(8,128)(4,1)S(1)} %copy-done.2), kind=kOutput, calls=%fused_computation.52 | output fusion | flops 12583423 | bytes 17055744 | tf_op jit(solution)/shard_map/sub | solution.py:39
  69.8 1.5 fusion.12
  71.3 1.3 fusion.1
  72.7 2.5 %fusion.3 = bf16[8,512,512]{1,2,0:T(8,128)(2,1)S(1)} fusion(f32[512,8,512]{2,0,1:T(8,128)S(1)} %get-tuple-element.57, f32[8,512]{1,0:T(8,128)S(1)} %get-tuple-element.56, f32[8,512,512]{1,2,0:T(8,128)S(1)} %get-tuple-element.55, f32[8,512]{1,0:T(8,128)S(1)} %get-tuple-element.54), kind=kLoop, calls=%fused_computation.5 | loop fusion | flops 8388608 | bytes 21004288 | tf_op jit(solution)/shard_map/convert_element_type | solution.py:45
  75.2 1.9 copy-done
  77.1 1.5 fusion.11
  78.7 0.2 copy.85
  78.9 0.4 broadcast_multiply_fusion
  79.3 27.0 %all-reduce.2 = bf16[512,2,256]{2,1,0:T(2,128)(2,1)S(1)} all-reduce(f32[512,2,256]{2,1,0:T(2,128)S(1)} %broadcast_multiply_fusion), channel_id=2, replica_groups=mesh['dp'=8,'seq'=4] {'seq'}, use_global_device_ids=true, to_apply=%region_5.6.clone | all-reduce | flops 262144 | bytes 1572864
  106.3 0.1 dynamic-slice_convert_fusion
  106.4 0.1 fusion.28
  106.6 7.4 %all_gather.10 = bf16[512,512]{1,0:T(8,128)(2,1)S(1)} all-gather(bf16[128,512]{1,0:T(8,128)(2,1)S(1)} %pad_maximum_fusion.2), channel_id=1, replica_groups=mesh['dp'=8,'seq'=4] {'seq'}, dimensions={0}, use_global_device_ids=true | all-gather | bytes 655360 | tf_op jit(solution)/shard_map/all_gather | solution.py:124
  114.0 2.1 %convolution_bitcast_fusion = f32[1024,512]{0,1:T(8,128)} fusion(bf16[512,512]{1,0:T(8,128)(2,1)S(1)} %all_gather.10, bf16[64,8,8,128]{3,2,1,0:T(8,128)(2,1)S(1)} %bitcast.94), kind=kOutput, calls=%fused_computation.16 | convolution fusion | flops 536870912 | bytes 3670016 | tf_op jit(solution)/shard_map/td,tc->dc/dot_general | solution.py:126
  116.1 0.0 reduce-scatter.2.cloned.1.call-update
  116.1 3.5 %fusion.10 = bf16[512,8,128]{2,0,1:T(8,128)(2,1)S(1)} fusion(bf16[8,512,512]{1,2,0:T(8,128)(2,1)} %copy-done, bf16[512,256]{1,0:T(8,128)(2,1)S(1)} %dynamic-slice_bitcast_fusion), kind=kOutput, calls=%fused_computation.17 | convolution fusion | flops 537919488 | bytes 5373952 | tf_op jit(solution)/shard_map/hqk,kd->hqd/dot_general | solution.py:48
  119.6 0.7 copy.78
  120.3 1.3 all_to_all.51
  121.6 3.5 %all-to-all-start.2 = ((bf16[4,128,1024]{2,1,0:T(8,128)(2,1)}), bf16[4,128,1024]{2,1,0:T(8,128)(2,1)S(1)}, u32[]{:S(2)}, u32[]{:S(2)}) async-start(bf16[4,128,1024]{2,1,0:T(8,128)(2,1)} %all_to_all.51), calls=%async_computation.2 | async-start | bytes 2097152 | tf_op jit(solution)/shard_map/all_to_all | solution.py:103
  125.1 0.1 copy.80
  125.3 14.3 %all-to-all-done.2 = bf16[4,128,1024]{2,1,0:T(8,128)(2,1)S(1)} async-done(((bf16[4,128,1024]{2,1,0:T(8,128)(2,1)}), bf16[4,128,1024]{2,1,0:T(8,128)(2,1)S(1)}, u32[]{:S(2)}, u32[]{:S(2)}) %all-to-all-start.2) | async-done | bytes 1048608 | tf_op jit(solution)/shard_map/all_to_all | solution.py:103
  139.5 0.7 copy.79
  140.2 1.3 copy.87
  141.5 43.9 %reduce-scatter.2.cloned.1.call-done = f32[128,512]{0,1:T(8,128)} async-done(((f32[1024,512]{0,1:T(8,128)}), f32[128,512]{0,1:T(8,128)}) %reduce-scatter.2.cloned.1.call-update) | async-done | bytes 262160 | tf_op jit(solution)/shard_map/reduce_scatter | solution.py:125
  185.4 1.0 multiply_reduce_fusion
  186.4 1.0 subtract_convert_fusion
  187.4 7.3 %all_gather.11 = bf16[512,512]{0,1:T(8,128)(2,1)S(1)} all-gather(bf16[128,512]{0,1:T(8,128)(2,1)S(1)} %subtract_convert_fusion), channel_id=1, replica_groups=mesh['dp'=8,'seq'=4] {'seq'}, dimensions={0}, use_global_device_ids=true | all-gather | bytes 655360 | tf_op jit(solution)/shard_map/all_gather | solution.py:135
  194.7 1.0 copy.88
  (24 shorter events, 0.2 us)
Async XLA Ops:
  7.2 28.7 %copy-start.6 = (u32[32]{0:T(128)S(1)}, u32[32]{0:T(128)}, u32[]{:S(2)}) copy-start(u32[32]{0:T(128)} %constant.125) | copy-start | bytes 388
  7.2 25.4 %copy-start.3 = (bf16[1,128,256]{2,1,0:T(8,128)(2,1)S(1)}, bf16[1,128,256]{2,1,0:T(8,128)(2,1)}, u32[]{:S(2)}) copy-start(bf16[1,128,256]{2,1,0:T(8,128)(2,1)} %param.17) | copy-start | bytes 196612
  7.2 25.5 %copy-start.4 = (bf16[1,128,256]{2,1,0:T(8,128)(2,1)S(1)}, bf16[1,128,256]{2,1,0:T(8,128)(2,1)}, u32[]{:S(2)}) copy-start(bf16[1,128,256]{2,1,0:T(8,128)(2,1)} %param.18) | copy-start | bytes 196612
  7.2 25.5 %copy-start.5 = (s32[1,8]{1,0:T(1,128)S(1)}, s32[1,8]{1,0:T(1,128)}, u32[]{:S(2)}) copy-start(s32[1,8]{1,0:T(1,128)} %param.20) | copy-start | bytes 100
  10.4 18.7 %all-to-all-start = ((bf16[128,4,1024]{2,0,1:T(8,128)(2,1)}), bf16[128,4,1024]{2,0,1:T(8,128)(2,1)S(1)}, u32[]{:S(2)}, u32[]{:S(2)}) async-start(bf16[128,4,1024]{2,0,1:T(8,128)(2,1)} %copy.73), calls=%async_computation | async-start | bytes 2097152 | tf_op jit(solution)/shard_map/all_to_all | solution.py:79
  29.1 22.8 %all-to-all-start.1 = ((bf16[128,4,1024]{2,0,1:T(8,128)(2,1)}), bf16[128,4,1024]{2,0,1:T(8,128)(2,1)S(1)}, u32[]{:S(2)}, u32[]{:S(2)}) async-start(bf16[128,4,1024]{2,0,1:T(8,128)(2,1)} %copy.75), calls=%async_computation.1 | async-start | bytes 2097152 | tf_op jit(solution)/shard_map/all_to_all | solution.py:80
  51.9 62.1 %all-to-all-start.3 = ((bf16[128,8,4,128]{3,1,0,2:T(8,128)(2,1)}), bf16[128,8,4,128]{3,1,0,2:T(8,128)(2,1)S(1)}, u32[]{:S(2)}, u32[]{:S(2)}) async-start(bf16[128,8,4,128]{3,1,0,2:T(8,128)(2,1)} %copy.86), calls=%async_computation.3 | async-start | bytes 2097152 | tf_op jit(solution)/shard_map/all_to_all | solution.py:121
  55.5 129.9 %reduce-scatter.2.cloned.1.call-start = ((), (), s32[]{:S(2)}) async-start(), calls=%async_computation.5 | async-start | bytes 2359296 | tf_op jit(solution)/shard_map/reduce_scatter | solution.py:125
  55.7 4.8 %copy-start.2 = (pred[512,512]{0,1:T(8,128)(4,1)S(1)}, pred[512,512]{0,1:T(8,128)(4,1)}, u32[]{:S(2)}) copy-start(pred[512,512]{0,1:T(8,128)(4,1)} %fusion.25) | copy-start | bytes 786436
  75.2 1.9 copy-start
  114.0 11.1 %copy-start.1 = (f32[128,512]{1,0:T(8,128)S(1)}, f32[128,512]{1,0:T(8,128)}, u32[]{:S(2)}) copy-start(f32[128,512]{1,0:T(8,128)} %param.21) | copy-start | bytes 786436
  121.6 18.0 %all-to-all-start.2 = ((bf16[4,128,1024]{2,1,0:T(8,128)(2,1)}), bf16[4,128,1024]{2,1,0:T(8,128)(2,1)S(1)}, u32[]{:S(2)}, u32[]{:S(2)}) async-start(bf16[4,128,1024]{2,1,0:T(8,128)(2,1)} %all_to_all.51), calls=%async_computation.2 | async-start | bytes 2097152 | tf_op jit(solution)/shard_map/all_to_all | solution.py:103
Sparse Core Ops, SparseCore 0:
  116.2 69.1 reduce-scatter.1
where the time goes:
time: 203 us
  waiting for transfers between devices  69.5 us (34%)
  blocking collectives  55.2 us (27%)
  local copies, waits for them, and re-layouts  17.8 us (9%)
  other arithmetic  15.5 us (8%)
  starting transfers between devices  15 us (7%)
  between operations  15 us (7%)
  matrix products  14.4 us (7%)
    reduce_scatter x1, waiting for transfers between devices, body(): lax.psum_scatter(jnp.einsum('td,tc->dc', regrouped, pair_all, preferred_e...  43.9 us
    unnamed x1, blocking collectives  27 us
    all_to_all x1, waiting for transfers between devices, body(): lax.all_to_all(query_local, 'seq', split_axis=0, concat_axis=1, tiled=True)  14.3 us
    all_gather x1, blocking collectives, body(): all_pairs = lax.all_gather(pairs, 'seq', axis=0, tiled=True)  13.5 us
    all_to_all x1, waiting for transfers between devices, body(): lax.all_to_all(query_send, 'seq', split_axis=1, concat_axis=0, tiled=True)  11.3 us
    sub x1, other arithmetic, group_grads(): shifted = jnp.exp(scores - jnp.max(scores, axis=2, keepdims=True))  9.31 us
    all_gather x1, blocking collectives, body(): pair_all = lax.all_gather(pair_grad, 'seq', axis=0, tiled=True)  7.43 us
    all_gather x1, blocking collectives, body(): gathered = lax.all_gather(fresh_rows, 'seq', axis=0, tiled=True)  7.25 us
  transfers between devices with their start and end apart: 5, of which 3 were waited for; matrix products, arithmetic and copies ran while one was open for 18% of the time, Pallas kernels for 0%

commit v1 on v0

v1 whole, which is shorter than its diff:
```python
import functools
import math

import jax
import jax.numpy as jnp
from jax import lax
from jax.experimental import pallas as pl
from jax.experimental.pallas import tpu as pltpu
from jax.sharding import PartitionSpec as P

KEY_VALUE_HEADS = 2
HEAD_SIZE = 128
learn_rate = 0.5
decay_rate = 0.1
F32 = jnp.float32
BF16 = jnp.bfloat16
MESH = pl.DeviceIdType.MESH


def contract(a, b, dim_a, dim_b):
    return lax.dot_general(a, b, (((dim_a,), (dim_b,)), ((), ())), preferred_element_type=F32)


def kernel(
    plan,
    seg_ref, hidden_ref, query_ref, key_ref, value_ref, grad_ref, weights_ref,
    query_out, updated_ref,
    q_vm, g_vm, dq_vm, k_buf, v_buf, kt_buf, bias_buf, dk_acc, dv_acc,
    part_out, part_in, hid_buf, hidt_buf, pair_buf, wg_buf, wg_half, rs_in, w_vm,
    local_sem, out_sem, kv_out, kv_in, hid_out, hid_in, part_send, part_recv,
    pair_out, pair_recv, fwd_out, fwd_recv, rs_send, rs_recv, up_out, up_recv, upf_out, upf_recv,
):
    S, G, NZ, T, R, W, strips, ndoc = (plan[n] for n in ("S", "G", "NZ", "T", "R", "W", "strips", "ndoc"))
    C = S // 2
    D = HEAD_SIZE
    heads = query_ref.shape[2] // D
    per_group = heads // KEY_VALUE_HEADS
    scale = D ** -0.5
    d = lax.axis_index("dp")
    s = lax.axis_index("seq")
    z, y = d // G, d % G
    chip, core = s // 2, s % 2
    sibling = (d, chip * 2 + 1 - core)

    def member(dy, dc, pc):
        to_core = core if pc == 0 else 1 - core
        return (z * G + (y + dy) % G, ((chip + dc) % C) * 2 + to_core)

    offsets = [(dy, dc, pc) for dy in range(G) for dc in range(C) for pc in range(2)]
    slot = {o: i for i, o in enumerate(offsets)}
    spread = [o for o in offsets if o[2] == 0]

    loads = [
        pltpu.make_async_copy(key_ref.at[0], k_buf.at[pl.ds(W * T, T)], local_sem.at[0]),
        pltpu.make_async_copy(value_ref.at[0], v_buf.at[pl.ds(W * T, T)], local_sem.at[1]),
        pltpu.make_async_copy(query_ref.at[0], q_vm, local_sem.at[2]),
        pltpu.make_async_copy(grad_ref.at[0], g_vm, local_sem.at[3]),
        pltpu.make_async_copy(weights_ref, w_vm, local_sem.at[4]),
    ]
    for copy in loads:
        copy.start()

    for back in range(1, W + 1):
        @pl.when(s < back)
        def _(back=back):
            k_buf[pl.ds((W - back) * T, T), :] = jnp.zeros((T, k_buf.shape[1]), BF16)
            v_buf[pl.ds((W - back) * T, T), :] = jnp.zeros((T, v_buf.shape[1]), BF16)

    barrier = pltpu.get_barrier_semaphore()
    peers = [member(*o) for o in offsets[1:]]
    peers += [(((z + dz) % NZ) * G + y, s) for dz in range(1, NZ)]
    for peer in peers:
        pl.semaphore_signal(barrier, inc=1, device_id=peer, device_id_type=MESH)
    pl.semaphore_wait(barrier, len(peers))

    def remote(src, dst, send, recv, peer):
        return pltpu.make_async_remote_copy(
            src_ref=src, dst_ref=dst, send_sem=send, recv_sem=recv,
            device_id=peer, device_id_type=MESH,
        )

    def kv_copies(back):
        to = (d, lax.rem(s + back, S))
        rows = pl.ds((W - back) * T, T)
        return [
            remote(key_ref.at[0], k_buf.at[rows], kv_out.at[0, back - 1], kv_in.at[0, back - 1], to),
            remote(value_ref.at[0], v_buf.at[rows], kv_out.at[1, back - 1], kv_in.at[1, back - 1], to),
        ]

    for back in range(1, W + 1):
        @pl.when(s + back < S)
        def _(back=back):
            for copy in kv_copies(back):
                copy.start()

    query_at = lax.broadcasted_iota(jnp.int32, (1, T), 1) + s * T
    first = jnp.zeros((1, T), jnp.int32)
    end = jnp.int32(0)
    for i in range(ndoc):
        length = seg_ref[0, i]
        end = end + length
        first = first + jnp.where(query_at >= end, length, 0)
    key_at = lax.broadcasted_iota(jnp.int32, ((W + 1) * T, T), 0) + (s - W) * T
    bias = jnp.where((key_at >= first) & (key_at <= query_at), 0.0, -1e30).astype(F32)
    bias_buf[:, :T] = bias
    bias_buf[:, T:] = bias

    def hid_dst(o, zz=None):
        rows = pl.ds(slot[o] * T, T)
        if zz is None:
            return hid_buf.at[rows]
        return hid_buf.at[rows, pl.ds(zz * R, R)]

    def hid_src(o, zz):
        dy, dc, pc = o
        to_d, to_s = member(*o)
        ty = (y + dy) % G
        if strips:
            column = pl.multiple_of(((zz * G + ty) * S + to_s) * R, 128)
            return hidden_ref.at[0, :, pl.ds(column, R)]
        return hidden_ref.at[ty * S + to_s]

    def hid_copies(o):
        i = slot[o]
        pieces = [(hid_src(o, zz), hid_dst(o, zz)) for zz in range(NZ)] if strips else [
            (hid_src(o, None), hid_dst(o))
        ]
        if i == 0:
            return [pltpu.make_async_copy(a, b, hid_in.at[0]) for a, b in pieces]
        return [remote(a, b, hid_out.at[i], hid_in.at[i], member(*o)) for a, b in pieces]

    def hid_whole(o, sem):
        return pltpu.make_async_copy(hid_dst(o), hid_dst(o), sem)

    for o in offsets:
        for copy in hid_copies(o):
            copy.start()

    for copy in loads:
        copy.wait()
    for back in range(1, W + 1):
        @pl.when(s >= back)
        def _(back=back):
            for copy in kv_copies(back):
                copy.wait_recv()

    def attention(g):
        columns = pl.ds(g * D, D)
        kt_buf[...] = k_buf[:, columns].T
        dk_acc[...] = jnp.zeros_like(dk_acc)
        dv_acc[...] = jnp.zeros_like(dv_acc)

        def pair(i, carry):
            at = pl.multiple_of((g * per_group + 2 * i) * D, 2 * D)
            q2 = q_vm[:, pl.ds(at, 2 * D)]
            q2 = jnp.concatenate([q2[:, :D], q2[:, D:]], axis=0)
            g2 = g_vm[:, pl.ds(at, 2 * D)]
            g2 = jnp.concatenate([g2[:, :D], g2[:, D:]], axis=0)
            scores = contract(k_buf[:, columns], q2, 1, 1)
            scores = scores * (scale * math.log2(math.e)) + bias_buf[...]
            shifted = jnp.exp2(scores - jnp.max(scores, axis=0, keepdims=True))
            attend = shifted * (1.0 / jnp.sum(shifted, axis=0, keepdims=True))
            prob_grad = contract(v_buf[:, columns], g2, 1, 1)
            delta = jnp.sum(attend * prob_grad, axis=0, keepdims=True)
            score_grad = (attend * (prob_grad - delta)).astype(BF16)
            dk_acc[...] += contract(score_grad, q2, 1, 0)
            dv_acc[...] += contract(attend.astype(BF16), g2, 1, 0)
            dq = (contract(kt_buf[...], score_grad, 1, 0) * scale).T.astype(BF16)
            dq_vm[:, pl.ds(at, 2 * D)] = jnp.concatenate([dq[:T], dq[T:]], axis=1)
            return carry

        lax.fori_loop(0, per_group // 2, pair, 0)

    def dq_copy(g):
        columns = pl.ds(g * per_group * D, per_group * D)
        return pltpu.make_async_copy(dq_vm.at[:, columns], query_out.at[0, :, columns], out_sem.at[g])

    def part_copy(g, back):
        to = (d, lax.rem(s - back + S, S))
        return remote(
            part_out.at[g, back - 1], part_in.at[g, back - 1],
            part_send.at[g, back - 1], part_recv.at[g, back - 1], to,
        )

    def send_parts(g):
        dq_copy(g).start()
        for back in range(1, W + 1):
            @pl.when(s >= back)
            def _(back=back):
                rows = pl.ds((W - back) * T, T)
                part_out[g, back - 1, :, :D] = dk_acc[rows, :].astype(BF16)
                part_out[g, back - 1, :, D:] = dv_acc[rows, :].astype(BF16)
                part_copy(g, back).start()

    def pair_copy(g, o):
        i = slot[o]
        return remote(
            pair_buf.at[g, pl.ds(0, T)], pair_buf.at[g, pl.ds(i * T, T)],
            pair_out.at[g, i], pair_recv.at[g, i], member(*o),
        )

    def forward_copy(g, o):
        i = slot[o]
        return remote(
            pair_buf.at[g, pl.ds(i * T, T)], pair_buf.at[g, pl.ds((i + 1) * T, T)],
            fwd_out.at[g, i], fwd_recv.at[g, i], sibling,
        )

    def own_sum(g):
        rows = pl.ds(W * T, T)
        return dk_acc[rows, :], dv_acc[rows, :]

    def send_pairs(g, own):
        dk, dv = own
        for back in range(1, W + 1):
            @pl.when(s + back < S)
            def _(back=back):
                part_copy(g, back).wait_recv()
            here = s + back < S
            got = part_in[g, back - 1]
            dk = dk + jnp.where(here, got[:, :D].astype(F32), 0.0)
            dv = dv + jnp.where(here, got[:, D:].astype(F32), 0.0)
        pair_buf[g, pl.ds(0, T), :D] = (dk * scale).astype(BF16)
        pair_buf[g, pl.ds(0, T), D:] = dv.astype(BF16)
        for o in spread[1:]:
            pair_copy(g, o).start()
        forward_copy(g, spread[0]).start()

    def forward_pairs(g):
        for o in spread[1:]:
            pair_copy(g, o).wait_recv()
            forward_copy(g, o).start()

    def rs_copy(g, dz):
        to = (z + dz) % NZ
        return remote(
            wg_half.at[g, pl.ds(pl.multiple_of(to * R, R), R)], rs_in.at[g, dz - 1],
            rs_send.at[g, dz - 1], rs_recv.at[g, dz - 1], (to * G + y, s),
        )

    def weight_part(g):
        for o in spread:
            forward_copy(g, o).wait_recv()
        total = contract(hidt_buf[...], pair_buf[g], 1, 0)
        wg_buf[g] = total
        wg_half[g] = total.astype(BF16)
        for dz in range(1, NZ):
            rs_copy(g, dz).start()

    for back in range(1, W + 1):
        @pl.when(s + back >= S)
        def _(back=back):
            for g in range(KEY_VALUE_HEADS):
                part_in[g, back - 1] = jnp.zeros(part_in.shape[2:], BF16)

    attention(0)
    send_parts(0)
    own = own_sum(0)
    send_pairs(0, own)
    attention(1)
    send_parts(1)
    forward_pairs(0)
    send_pairs(1, own_sum(1))
    for o in offsets:
        hid_whole(o, hid_in.at[slot[o]]).wait()
        rows = pl.ds(slot[o] * T, T)
        hidt_buf[:, rows] = hid_buf[rows, :].T
    weight_part(0)
    forward_pairs(1)
    weight_part(1)

    mine = pl.ds(pl.multiple_of(z * R, R), R)
    grads = []
    for g in range(KEY_VALUE_HEADS):
        total = wg_buf[g, mine, :]
        for dz in range(1, NZ):
            rs_copy(g, dz).wait_recv()
            total = total + rs_in[g, dz - 1].astype(F32)
        grads.append(total)
    width = weights_ref.shape[1]
    square = sum(jnp.sum(t * t, axis=1, keepdims=True) for t in grads)
    factor = learn_rate / jnp.sqrt(square * (1.0 / width) + 1e-6)
    keep = 1.0 - learn_rate * decay_rate

    def rows_of(owner):
        return pl.ds(pl.multiple_of(owner * R, R), R)

    for g in range(KEY_VALUE_HEADS):
        for kind in range(2):
            columns = pl.ds((kind * KEY_VALUE_HEADS + g) * D, D)
            updated_ref[rows_of(s), columns] = (
                w_vm[:, columns] * keep - grads[g][:, kind * D : (kind + 1) * D] * factor
            ).astype(BF16)

    def up_copy(dc):
        rows = updated_ref.at[rows_of(s)]
        return remote(rows, rows, up_out.at[dc], up_recv.at[dc], (d, ((chip + dc) % C) * 2 + core))

    def up_forward(dc):
        origin = ((chip + C - dc) % C) * 2 + core
        rows = updated_ref.at[rows_of(origin)]
        return remote(rows, rows, upf_out.at[dc], upf_recv.at[dc], sibling)

    for dc in range(1, C):
        up_copy(dc).start()
    up_forward(0).start()
    for dc in range(1, C):
        up_copy(dc).wait_recv()
        up_forward(dc).start()
    for dc in range(C):
        up_forward(dc).wait_recv()

    for dc in range(C):
        if dc:
            up_copy(dc).wait_send()
        up_forward(dc).wait_send()
    for back in range(1, W + 1):
        @pl.when(s + back < S)
        def _(back=back):
            for copy in kv_copies(back):
                copy.wait_send()

        @pl.when(s >= back)
        def _(back=back):
            for g in range(KEY_VALUE_HEADS):
                part_copy(g, back).wait_send()
    for o in offsets[1:]:
        hid_whole(o, hid_out.at[slot[o]]).wait()
    for g in range(KEY_VALUE_HEADS):
        for o in spread:
            if slot[o]:
                pair_copy(g, o).wait_send()
            forward_copy(g, o).wait_send()
        for dz in range(1, NZ):
            rs_copy(g, dz).wait_send()
        dq_copy(g).wait()


def body(hidden, query_states, keys, values, out_grad, seg_lengths, weights):
    S = lax.axis_size("seq")
    dp = lax.axis_size("dp")
    G = 2 if dp % 2 == 0 else 1
    NZ = dp // G
    C = S // 2
    T = hidden.shape[1]
    R, width = weights.shape
    W = S // 2
    D = HEAD_SIZE
    KV = KEY_VALUE_HEADS
    members = G * S
    strips = R % 128 == 0
    if not strips:
        hidden = hidden[0].reshape(T, NZ, G, S, R).transpose(2, 3, 0, 1, 4).reshape(members, T, NZ * R)
    plan = dict(S=S, G=G, NZ=NZ, T=T, R=R, W=W, strips=strips, ndoc=seg_lengths.shape[1])
    window = (W + 1) * T
    model = query_states.shape[2]
    dma = pltpu.SemaphoreType.DMA
    any_spec = pl.BlockSpec(memory_space=pl.ANY)
    scratch = [
        pltpu.VMEM((T, model), BF16),
        pltpu.VMEM((T, model), BF16),
        pltpu.VMEM((T, model), BF16),
        pltpu.VMEM((window, KV * D), BF16),
        pltpu.VMEM((window, KV * D), BF16),
        pltpu.VMEM((D, window), BF16),
        pltpu.VMEM((window, 2 * T), F32),
        pltpu.VMEM((window, D), F32),
        pltpu.VMEM((window, D), F32),
        pltpu.VMEM((KV, W, T, 2 * D), BF16),
        pltpu.VMEM((KV, W, T, 2 * D), BF16),
        pltpu.VMEM((members * T, NZ * R), BF16),
        pltpu.VMEM((NZ * R, members * T), BF16),
        pltpu.VMEM((KV, members * T, 2 * D), BF16),
        pltpu.VMEM((KV, NZ * R, 2 * D), F32),
        pltpu.VMEM((KV, NZ * R, 2 * D), BF16),
        pltpu.VMEM((KV, max(NZ - 1, 1), R, 2 * D), BF16),
        pltpu.VMEM((R, width), F32),
        dma((5,)), dma((KV,)), dma((2, W)), dma((2, W)), dma((members,)), dma((members,)),
        dma((KV, W)), dma((KV, W)), dma((KV, members)), dma((KV, members)),
        dma((KV, members)), dma((KV, members)),
        dma((KV, max(NZ - 1, 1))), dma((KV, max(NZ - 1, 1))),
        dma((C,)), dma((C,)), dma((C,)), dma((C,)),
    ]
    return pl.pallas_call(
        functools.partial(kernel, plan),
        out_shape=(
            jax.ShapeDtypeStruct(query_states.shape, BF16),
            jax.ShapeDtypeStruct((S * R, width), BF16),
        ),
        in_specs=[pl.BlockSpec(memory_space=pltpu.SMEM)] + [any_spec] * 6,
        out_specs=(any_spec, pl.BlockSpec(memory_space=pltpu.VMEM)),
        scratch_shapes=scratch,
        compiler_params=pltpu.CompilerParams(
            collective_id=0, has_side_effects=True, vmem_limit_bytes=56 * 1024 * 1024
        ),
    )(seg_lengths, hidden, query_states, keys, values, out_grad, weights)


def solution(mesh):
    placed = (
        P("dp", "seq", None),
        P("dp", "seq", None),
        P("dp", "seq", None),
        P("dp", "seq", None),
        P("dp", "seq", None),
        P("dp", None),
        P(("dp", "seq"), None),
    )
    return jax.shard_map(
        body,
        mesh=mesh,
        in_specs=placed,
        out_specs=(P("dp", "seq", None), P("dp", None)),
        check_vma=False,
    )
```

time: 203 us -> 54.6 us (0.27)
  waiting for transfers between devices: 69.5 us -> 0 us
  blocking collectives: 55.2 us -> 0 us
  Pallas kernels: 0 us -> 50 us
  other arithmetic: 15.5 us -> 0 us
  starting transfers between devices: 15 us -> 0 us
  local copies, waits for them, and re-layouts: 17.8 us -> 3.14 us
  matrix products: 14.4 us -> 0 us
  between operations: 15 us -> 0.65 us
    pallas_call x0 -> x1, Pallas kernels: none -> 50 us  [body(): pl.pallas_call(functools.partial(kernel, plan), out_shape=(jax.ShapeDtype...]
    reduce_scatter x1 -> x0, waiting for transfers between devices: 43.9 us -> none  [body(): lax.psum_scatter(jnp.einsum('td,tc->dc', regrouped, pair_all, preferred_e...]
    all_gather x3 -> x0, blocking collectives: 28.2 us -> none  [the longest x1 13.5 us: body(): all_pairs = lax.all_gather(pairs, 'seq', axis=0, tiled=True)]
    unnamed x1 -> x0, blocking collectives: 27 us -> none
    all_to_all x4 -> x0, waiting for transfers between devices: 25.6 us -> none  [the longest x1 14.3 us: body(): lax.all_to_all(query_local, 'seq', split_axis=0, concat_axis=1, tiled=True)]
    all_to_all x4 -> x0, starting transfers between devices: 14.8 us -> none  [the longest x1 4.21 us: body(): lax.all_to_all(query_send, 'seq', split_axis=1, concat_axis=0, tiled=True)]
    dot_general x6 -> x0, matrix products: 14.4 us -> none  [the longest x1 4.49 us: group_grads(): jnp.einsum('hqd,kd->hqk', query_block, key_rows, preferred_element_type=j...]
    another operation x11 -> x0, local copies, waits for them, and re-layouts: 9.39 us -> none  [the longest x2 3.18 us: body(): query_states[0].reshape(token_rows, sequence_count, local_heads * HEAD_SIZE)]
  transfers between devices with their start and end apart: 5 -> 0, of which waited for: 3 -> 0; matrix products, arithmetic and copies ran while one was open for 18% -> 0% of each run, Pallas kernels for 0% -> 0%
where the time goes in v1:
time: 54.6 us; the launch traced here: 53.8 us
  Pallas kernels  50 us (92%)
  local copies, waits for them, and re-layouts  3.14 us (6%)
  between operations  0.65 us (1%)
    pallas_call x1, Pallas kernels, body(): pl.pallas_call(functools.partial(kernel, plan), out_shape=(jax.ShapeDtype...  50 us
    unnamed x4, local copies, waits for them, and re-layouts  3.14 us

profile of v1, /device:TPU:0, one launch (start us, length us, event | category | flops | bytes accessed | tf_op | source)
XLA Modules:
  0.0 53.8 jit_solution(7209309727346457606)
XLA Ops:
  0.6 50.0 %shard_map.86 = (bf16[1,128,4096]{2,1,0:T(8,128)(2,1)}, bf16[512,512]{1,0:T(8,128)(2,1)}) custom-call(s32[1,8]{1,0:T(1,128)} %seg_ref.1, bf16[1,128,4096]{2,1,0:T(8,128)(2,1)} %hidden_ref.1, bf16[1,128,4096]{2,1,0:T(8,128)(2,1)} %query_ref.1, bf16[1,128,256]{2,1,0:T(8,128)(2,1)} %key_ref.1, bf16[1,128,256]{2,1,0:T(8,128)(2,1)} %value_ref.1, ...), custom_call_target="tpu_custom_call" | custom-call | tf_op jit(solution)/shard_map/pallas_call | solution.py:384
  50.6 0.0 copy-start
  50.6 2.3 %copy.11 = bf16[1,128,4096]{2,1,0:T(8,128)(2,1)} copy(bf16[1,128,4096]{2,1,0:T(8,128)(2,1)} %get-tuple-element.4) | data formatting | bytes 2097152
  53.0 0.0 copy-done
  53.0 0.8 %copy.12 = bf16[512,512]{1,0:T(8,128)(2,1)} copy(bf16[512,512]{1,0:T(8,128)(2,1)S(1)} %copy-done) | data formatting | bytes 1048576
Async XLA Ops:
  50.6 2.4 %copy-start = (bf16[512,512]{1,0:T(8,128)(2,1)S(1)}, bf16[512,512]{1,0:T(8,128)(2,1)}, u32[]{:S(2)}) copy-start(bf16[512,512]{1,0:T(8,128)(2,1)} %get-tuple-element.5) | copy-start | bytes 1572868

commit v2 on v1

--- a/solution.py
+++ b/solution.py
@@ -30,7 +30,10 @@
     local_sem, out_sem, kv_out, kv_in, hid_out, hid_in, part_send, part_recv,
     pair_out, pair_recv, fwd_out, fwd_recv, rs_send, rs_recv, up_out, up_recv, upf_out, upf_recv,
 ):
-    S, G, NZ, T, R, W, strips, ndoc = (plan[n] for n in ("S", "G", "NZ", "T", "R", "W", "strips", "ndoc"))
+    S, G, NZ, T, R, W, H, strips, ndoc = (
+        plan[n] for n in ("S", "G", "NZ", "T", "R", "W", "H", "strips", "ndoc")
+    )
+    Rh = R // H
     C = S // 2
     D = HEAD_SIZE
     heads = query_ref.shape[2] // D
@@ -79,19 +82,24 @@
             device_id=peer, device_id_type=MESH,
         )
 
-    def kv_copies(back):
+    def kv_copies(g, back):
         to = (d, lax.rem(s + back, S))
         rows = pl.ds((W - back) * T, T)
+        cols = pl.ds(g * D, D)
         return [
-            remote(key_ref.at[0], k_buf.at[rows], kv_out.at[0, back - 1], kv_in.at[0, back - 1], to),
-            remote(value_ref.at[0], v_buf.at[rows], kv_out.at[1, back - 1], kv_in.at[1, back - 1], to),
+            remote(
+                src.at[0, :, cols], dst.at[rows, cols],
+                kv_out.at[i, g, back - 1], kv_in.at[i, g, back - 1], to,
+            )
+            for i, (src, dst) in enumerate(((key_ref, k_buf), (value_ref, v_buf)))
         ]
 
-    for back in range(1, W + 1):
-        @pl.when(s + back < S)
-        def _(back=back):
-            for copy in kv_copies(back):
-                copy.start()
+    for g in range(KEY_VALUE_HEADS):
+        for back in range(W, 0, -1):
+            @pl.when(s + back < S)
+            def _(g=g, back=back):
+                for copy in kv_copies(g, back):
+                    copy.start()
 
     query_at = lax.broadcasted_iota(jnp.int32, (1, T), 1) + s * T
     first = jnp.zeros((1, T), jnp.int32)
@@ -138,17 +146,19 @@
 
     for copy in loads:
         copy.wait()
-    for back in range(1, W + 1):
-        @pl.when(s >= back)
-        def _(back=back):
-            for copy in kv_copies(back):
-                copy.wait_recv()
-
-    def attention(g):
+
+    def receive_keys(g):
+        for back in range(1, W + 1):
+            @pl.when(s >= back)
+            def _(back=back):
+                for copy in kv_copies(g, back):
+                    copy.wait_recv()
+        kt_buf[...] = k_buf[:, pl.ds(g * D, D)].T
+        dk_acc[g] = jnp.zeros(dk_acc.shape[1:], F32)
+        dv_acc[g] = jnp.zeros(dv_acc.shape[1:], F32)
+
+    def attention(g, begin, stop):
         columns = pl.ds(g * D, D)
-        kt_buf[...] = k_buf[:, columns].T
-        dk_acc[...] = jnp.zeros_like(dk_acc)
-        dv_acc[...] = jnp.zeros_like(dv_acc)
 
         def pair(i, carry):
             at = pl.multiple_of((g * per_group + 2 * i) * D, 2 * D)
@@ -163,13 +173,13 @@
             prob_grad = contract(v_buf[:, columns], g2, 1, 1)
             delta = jnp.sum(attend * prob_grad, axis=0, keepdims=True)
             score_grad = (attend * (prob_grad - delta)).astype(BF16)
-            dk_acc[...] += contract(score_grad, q2, 1, 0)
-            dv_acc[...] += contract(attend.astype(BF16), g2, 1, 0)
+            dk_acc[g] += contract(score_grad, q2, 1, 0)
+            dv_acc[g] += contract(attend.astype(BF16), g2, 1, 0)
             dq = (contract(kt_buf[...], score_grad, 1, 0) * scale).T.astype(BF16)
             dq_vm[:, pl.ds(at, 2 * D)] = jnp.concatenate([dq[:T], dq[T:]], axis=1)
             return carry
 
-        lax.fori_loop(0, per_group // 2, pair, 0)
+        lax.fori_loop(begin, stop, pair, 0)
 
     def dq_copy(g):
         columns = pl.ds(g * per_group * D, per_group * D)
@@ -188,8 +198,8 @@
             @pl.when(s >= back)
             def _(back=back):
                 rows = pl.ds((W - back) * T, T)
-                part_out[g, back - 1, :, :D] = dk_acc[rows, :].astype(BF16)
-                part_out[g, back - 1, :, D:] = dv_acc[rows, :].astype(BF16)
+                part_out[g, back - 1, :, :D] = dk_acc[g, rows, :].astype(BF16)
+                part_out[g, back - 1, :, D:] = dv_acc[g, rows, :].astype(BF16)
                 part_copy(g, back).start()
 
     def pair_copy(g, o):
@@ -208,7 +218,7 @@
 
     def own_sum(g):
         rows = pl.ds(W * T, T)
-        return dk_acc[rows, :], dv_acc[rows, :]
+        return dk_acc[g, rows, :], dv_acc[g, rows, :]
 
     def send_pairs(g, own):
         dk, dv = own
@@ -231,11 +241,12 @@
             pair_copy(g, o).wait_recv()
             forward_copy(g, o).start()
 
-    def rs_copy(g, dz):
+    def rs_copy(g, h, dz):
         to = (z + dz) % NZ
+        rows = pl.ds(pl.multiple_of(to * R + h * Rh, Rh), Rh)
         return remote(
-            wg_half.at[g, pl.ds(pl.multiple_of(to * R, R), R)], rs_in.at[g, dz - 1],
-            rs_send.at[g, dz - 1], rs_recv.at[g, dz - 1], (to * G + y, s),
+            wg_half.at[g, rows], rs_in.at[g, dz - 1, pl.ds(h * Rh, Rh)],
+            rs_send.at[g, h, dz - 1], rs_recv.at[g, h, dz - 1], (to * G + y, s),
         )
 
     def weight_part(g):
@@ -244,8 +255,9 @@
         total = contract(hidt_buf[...], pair_buf[g], 1, 0)
         wg_buf[g] = total
         wg_half[g] = total.astype(BF16)
-        for dz in range(1, NZ):
-            rs_copy(g, dz).start()
+        for h in range(H):
+            for dz in range(1, NZ):
+                rs_copy(g, h, dz).start()
 
     for back in range(1, W + 1):
         @pl.when(s + back >= S)
@@ -253,72 +265,81 @@
             for g in range(KEY_VALUE_HEADS):
                 part_in[g, back - 1] = jnp.zeros(part_in.shape[2:], BF16)
 
-    attention(0)
+    pairs = per_group // 2
+    middle = pairs * 5 // 8
+    receive_keys(0)
+    attention(0, 0, pairs)
     send_parts(0)
-    own = own_sum(0)
-    send_pairs(0, own)
-    attention(1)
+    receive_keys(1)
+    attention(1, 0, middle)
+    send_pairs(0, own_sum(0))
+    attention(1, middle, pairs)
     send_parts(1)
-    forward_pairs(0)
-    send_pairs(1, own_sum(1))
     for o in offsets:
         hid_whole(o, hid_in.at[slot[o]]).wait()
         rows = pl.ds(slot[o] * T, T)
         hidt_buf[:, rows] = hid_buf[rows, :].T
+    send_pairs(1, own_sum(1))
+    forward_pairs(0)
     weight_part(0)
     forward_pairs(1)
     weight_part(1)
 
-    mine = pl.ds(pl.multiple_of(z * R, R), R)
-    grads = []
-    for g in range(KEY_VALUE_HEADS):
-        total = wg_buf[g, mine, :]
-        for dz in range(1, NZ):
-            rs_copy(g, dz).wait_recv()
-            total = total + rs_in[g, dz - 1].astype(F32)
-        grads.append(total)
     width = weights_ref.shape[1]
-    square = sum(jnp.sum(t * t, axis=1, keepdims=True) for t in grads)
-    factor = learn_rate / jnp.sqrt(square * (1.0 / width) + 1e-6)
     keep = 1.0 - learn_rate * decay_rate
 
-    def rows_of(owner):
-        return pl.ds(pl.multiple_of(owner * R, R), R)
-
-    for g in range(KEY_VALUE_HEADS):
-        for kind in range(2):
-            columns = pl.ds((kind * KEY_VALUE_HEADS + g) * D, D)
-            updated_ref[rows_of(s), columns] = (
-                w_vm[:, columns] * keep - grads[g][:, kind * D : (kind + 1) * D] * factor
-            ).astype(BF16)
-
-    def up_copy(dc):
-        rows = updated_ref.at[rows_of(s)]
-        return remote(rows, rows, up_out.at[dc], up_recv.at[dc], (d, ((chip + dc) % C) * 2 + core))
-
-    def up_forward(dc):
+    def rows_of(owner, h):
+        return pl.ds(pl.multiple_of(owner * R + h * Rh, Rh), Rh)
+
+    def up_copy(h, dc):
+        rows = updated_ref.at[rows_of(s, h)]
+        to = (d, ((chip + dc) % C) * 2 + core)
+        return remote(rows, rows, up_out.at[h, dc], up_recv.at[h, dc], to)
+
+    def up_forward(h, dc):
         origin = ((chip + C - dc) % C) * 2 + core
-        rows = updated_ref.at[rows_of(origin)]
-        return remote(rows, rows, upf_out.at[dc], upf_recv.at[dc], sibling)
-
-    for dc in range(1, C):
-        up_copy(dc).start()
-    up_forward(0).start()
-    for dc in range(1, C):
-        up_copy(dc).wait_recv()
-        up_forward(dc).start()
-    for dc in range(C):
-        up_forward(dc).wait_recv()
-
-    for dc in range(C):
-        if dc:
-            up_copy(dc).wait_send()
-        up_forward(dc).wait_send()
+        rows = updated_ref.at[rows_of(origin, h)]
+        return remote(rows, rows, upf_out.at[h, dc], upf_recv.at[h, dc], sibling)
+
+    for h in range(H):
+        grads = []
+        for g in range(KEY_VALUE_HEADS):
+            total = wg_buf[g, rows_of(z, h), :]
+            for dz in range(1, NZ):
+                rs_copy(g, h, dz).wait_recv()
+                total = total + rs_in[g, dz - 1, pl.ds(h * Rh, Rh)].astype(F32)
+            grads.append(total)
+        square = sum(jnp.sum(t * t, axis=1, keepdims=True) for t in grads)
+        factor = learn_rate / jnp.sqrt(square * (1.0 / width) + 1e-6)
+        for g in range(KEY_VALUE_HEADS):
+            for kind in range(2):
+                columns = pl.ds((kind * KEY_VALUE_HEADS + g) * D, D)
+                updated_ref[rows_of(s, h), columns] = (
+                    w_vm[pl.ds(h * Rh, Rh), columns] * keep
+                    - grads[g][:, kind * D : (kind + 1) * D] * factor
+                ).astype(BF16)
+        for dc in range(1, C):
+            up_copy(h, dc).start()
+        up_forward(h, 0).start()
+    for h in range(H):
+        for dc in range(1, C):
+            up_copy(h, dc).wait_recv()
+            up_forward(h, dc).start()
+    for h in range(H):
+        for dc in range(C):
+            up_forward(h, dc).wait_recv()
+
+    for h in range(H):
+        for dc in range(C):
+            if dc:
+                up_copy(h, dc).wait_send()
+            up_forward(h, dc).wait_send()
     for back in range(1, W + 1):
         @pl.when(s + back < S)
         def _(back=back):
-            for copy in kv_copies(back):
-                copy.wait_send()
+            for g in range(KEY_VALUE_HEADS):
+                for copy in kv_copies(g, back):
+                    copy.wait_send()
 
         @pl.when(s >= back)
         def _(back=back):
@@ -331,8 +352,9 @@
             if slot[o]:
                 pair_copy(g, o).wait_send()
             forward_copy(g, o).wait_send()
-        for dz in range(1, NZ):
-            rs_copy(g, dz).wait_send()
+        for h in range(H):
+            for dz in range(1, NZ):
+                rs_copy(g, h, dz).wait_send()
         dq_copy(g).wait()
 
 
@@ -351,7 +373,8 @@
     strips = R % 128 == 0
     if not strips:
         hidden = hidden[0].reshape(T, NZ, G, S, R).transpose(2, 3, 0, 1, 4).reshape(members, T, NZ * R)
-    plan = dict(S=S, G=G, NZ=NZ, T=T, R=R, W=W, strips=strips, ndoc=seg_lengths.shape[1])
+    H = 2 if R % 32 == 0 else 1
+    plan = dict(S=S, G=G, NZ=NZ, T=T, R=R, W=W, H=H, strips=strips, ndoc=seg_lengths.shape[1])
     window = (W + 1) * T
     model = query_states.shape[2]
     dma = pltpu.SemaphoreType.DMA
@@ -364,8 +387,8 @@
         pltpu.VMEM((window, KV * D), BF16),
         pltpu.VMEM((D, window), BF16),
         pltpu.VMEM((window, 2 * T), F32),
-        pltpu.VMEM((window, D), F32),
-        pltpu.VMEM((window, D), F32),
+        pltpu.VMEM((KV, window, D), F32),
+        pltpu.VMEM((KV, window, D), F32),
         pltpu.VMEM((KV, W, T, 2 * D), BF16),
         pltpu.VMEM((KV, W, T, 2 * D), BF16),
         pltpu.VMEM((members * T, NZ * R), BF16),
@@ -375,11 +398,11 @@
         pltpu.VMEM((KV, NZ * R, 2 * D), BF16),
         pltpu.VMEM((KV, max(NZ - 1, 1), R, 2 * D), BF16),
         pltpu.VMEM((R, width), F32),
-        dma((5,)), dma((KV,)), dma((2, W)), dma((2, W)), dma((members,)), dma((members,)),
+        dma((5,)), dma((KV,)), dma((2, KV, W)), dma((2, KV, W)), dma((members,)), dma((members,)),
         dma((KV, W)), dma((KV, W)), dma((KV, members)), dma((KV, members)),
         dma((KV, members)), dma((KV, members)),
-        dma((KV, max(NZ - 1, 1))), dma((KV, max(NZ - 1, 1))),
-        dma((C,)), dma((C,)), dma((C,)), dma((C,)),
+        dma((KV, H, max(NZ - 1, 1))), dma((KV, H, max(NZ - 1, 1))),
+        dma((H, C)), dma((H, C)), dma((H, C)), dma((H, C)),
     ]
     return pl.pallas_call(
         functools.partial(kernel, plan),

time: 54.6 us -> 51.4 us (0.941)
  the two profiles are of different devices: /device:TPU:0 before, /device:TPU:3 now
where the time goes in v2:
time: 51.4 us; the launch traced here: 51.2 us
  Pallas kernels  47.4 us (92%)
  local copies, waits for them, and re-layouts  3.14 us (6%)
  between operations  0.65 us (1%)
    pallas_call x1, Pallas kernels, body(): pl.pallas_call(functools.partial(kernel, plan), out_shape=(jax.ShapeDtype...  47.4 us
    unnamed x4, local copies, waits for them, and re-layouts  3.14 us

profile of v2, /device:TPU:3, one launch (start us, length us, event | category | flops | bytes accessed | tf_op | source)
XLA Modules:
  0.0 51.2 jit_solution(9524332894744473745)
XLA Ops:
  0.6 47.4 %shard_map.86 = (bf16[1,128,4096]{2,1,0:T(8,128)(2,1)}, bf16[512,512]{1,0:T(8,128)(2,1)}) custom-call(s32[1,8]{1,0:T(1,128)} %seg_ref.1, bf16[1,128,4096]{2,1,0:T(8,128)(2,1)} %hidden_ref.1, bf16[1,128,4096]{2,1,0:T(8,128)(2,1)} %query_ref.1, bf16[1,128,256]{2,1,0:T(8,128)(2,1)} %key_ref.1, bf16[1,128,256]{2,1,0:T(8,128)(2,1)} %value_ref.1, ...), custom_call_target="tpu_custom_call" | custom-call | tf_op jit(solution)/shard_map/pallas_call | solution.py:407
  48.1 0.0 copy-start
  48.1 2.3 %copy.11 = bf16[1,128,4096]{2,1,0:T(8,128)(2,1)} copy(bf16[1,128,4096]{2,1,0:T(8,128)(2,1)} %get-tuple-element.4) | data formatting | bytes 2097152
  50.4 0.0 copy-done
  50.4 0.8 %copy.12 = bf16[512,512]{1,0:T(8,128)(2,1)} copy(bf16[512,512]{1,0:T(8,128)(2,1)S(1)} %copy-done) | data formatting | bytes 1048576
Async XLA Ops:
  48.1 2.4 %copy-start = (bf16[512,512]{1,0:T(8,128)(2,1)S(1)}, bf16[512,512]{1,0:T(8,128)(2,1)}, u32[]{:S(2)}) copy-start(bf16[512,512]{1,0:T(8,128)(2,1)} %get-tuple-element.5) | copy-start | bytes 1572868

commit v3 on v2

--- a/solution.py
+++ b/solution.py
@@ -275,12 +275,12 @@
     send_pairs(0, own_sum(0))
     attention(1, middle, pairs)
     send_parts(1)
+    send_pairs(1, own_sum(1))
+    forward_pairs(0)
     for o in offsets:
         hid_whole(o, hid_in.at[slot[o]]).wait()
         rows = pl.ds(slot[o] * T, T)
         hidt_buf[:, rows] = hid_buf[rows, :].T
-    send_pairs(1, own_sum(1))
-    forward_pairs(0)
     weight_part(0)
     forward_pairs(1)
     weight_part(1)
@@ -356,6 +356,19 @@
             for dz in range(1, NZ):
                 rs_copy(g, h, dz).wait_send()
         dq_copy(g).wait()
+
+
+def place(query_in, updated_in, query_out, updated_out, sem):
+    rows = query_in.shape[1] // 8
+    copies = [
+        pltpu.make_async_copy(query_in.at[0, pl.ds(i * rows, rows)], query_out.at[0, pl.ds(i * rows, rows)], sem.at[i])
+        for i in range(8)
+    ]
+    copies.append(pltpu.make_async_copy(updated_in, updated_out, sem.at[8]))
+    for copy in copies:
+        copy.start()
+    for copy in copies:
+        copy.wait()
 
 
 def body(hidden, query_states, keys, values, out_grad, seg_lengths, weights):
@@ -404,7 +417,7 @@
         dma((KV, H, max(NZ - 1, 1))), dma((KV, H, max(NZ - 1, 1))),
         dma((H, C)), dma((H, C)), dma((H, C)), dma((H, C)),
     ]
-    return pl.pallas_call(
+    outs = pl.pallas_call(
         functools.partial(kernel, plan),
         out_shape=(
             jax.ShapeDtypeStruct(query_states.shape, BF16),
@@ -417,6 +430,13 @@
             collective_id=0, has_side_effects=True, vmem_limit_bytes=56 * 1024 * 1024
         ),
     )(seg_lengths, hidden, query_states, keys, values, out_grad, weights)
+    return pl.pallas_call(
+        place,
+        out_shape=tuple(jax.ShapeDtypeStruct(o.shape, o.dtype) for o in outs),
+        in_specs=[pl.BlockSpec(memory_space=pltpu.VMEM)] * 2,
+        out_specs=(any_spec,) * 2,
+        scratch_shapes=[dma((9,))],
+    )(*outs)
 
 
 def solution(mesh):

time: 51.4 us -> 51.8 us (level)
  the two profiles are of different devices: /device:TPU:3 before, /device:TPU:0 now
where the time goes in v3:
time: 51.8 us; the launch traced here: 50.9 us
  Pallas kernels  50.2 us (97%)
  between operations  0.64 us (1%)
    pallas_call x1, Pallas kernels, body(): pl.pallas_call(functools.partial(kernel, plan), out_shape=(jax.ShapeDtype...  47.7 us
    pallas_call x1, Pallas kernels, body(): pl.pallas_call(place, out_shape=tuple((jax.ShapeDtypeStruct(o.shape, o.dt...  2.57 us

profile of v3, /device:TPU:0, one launch (start us, length us, event | category | flops | bytes accessed | tf_op | source)
XLA Modules:
  0.0 50.9 jit_solution(11989392214394487172)
XLA Ops:
  0.6 47.7 %shard_map.86 = (bf16[1,128,4096]{2,1,0:T(8,128)(2,1)}, bf16[512,512]{1,0:T(8,128)(2,1)}) custom-call(s32[1,8]{1,0:T(1,128)} %seg_ref.1, bf16[1,128,4096]{2,1,0:T(8,128)(2,1)} %hidden_ref.1, bf16[1,128,4096]{2,1,0:T(8,128)(2,1)} %query_ref.1, bf16[1,128,256]{2,1,0:T(8,128)(2,1)} %key_ref.1, bf16[1,128,256]{2,1,0:T(8,128)(2,1)} %value_ref.1, ...), custom_call_target="tpu_custom_call" | custom-call | tf_op jit(solution)/shard_map/pallas_call | solution.py:420
  48.3 2.6 %shard_map.87 = (bf16[1,128,4096]{2,1,0:T(8,128)(2,1)}, bf16[512,512]{1,0:T(8,128)(2,1)}) custom-call(bf16[1,128,4096]{2,1,0:T(8,128)(2,1)} %get-tuple-element.4.query_in, bf16[512,512]{1,0:T(8,128)(2,1)} %get-tuple-element.5.updated_in), custom_call_target="tpu_custom_call" | custom-call | tf_op jit(solution)/shard_map/pallas_call | solution.py:433

commit v4 on v2

--- a/solution.py
+++ b/solution.py
@@ -179,7 +179,7 @@
             dq_vm[:, pl.ds(at, 2 * D)] = jnp.concatenate([dq[:T], dq[T:]], axis=1)
             return carry
 
-        lax.fori_loop(begin, stop, pair, 0)
+        lax.fori_loop(begin, stop, pair, 0, unroll=2)
 
     def dq_copy(g):
         columns = pl.ds(g * per_group * D, per_group * D)
@@ -266,7 +266,7 @@
                 part_in[g, back - 1] = jnp.zeros(part_in.shape[2:], BF16)
 
     pairs = per_group // 2
-    middle = pairs * 5 // 8
+    middle = pairs // 2
     receive_keys(0)
     attention(0, 0, pairs)
     send_parts(0)

time: 51.4 us -> 52 us (1.012)
  the two profiles are of different devices: /device:TPU:3 before, /device:TPU:0 now
where the time goes in v4:
time: 52 us; the launch traced here: 51.8 us
  Pallas kernels  48.1 us (92%)
  local copies, waits for them, and re-layouts  3.14 us (6%)
  between operations  0.65 us (1%)
    pallas_call x1, Pallas kernels, body(): pl.pallas_call(functools.partial(kernel, plan), out_shape=(jax.ShapeDtype...  48.1 us
    unnamed x4, local copies, waits for them, and re-layouts  3.14 us

profile of v4, /device:TPU:0, one launch (start us, length us, event | category | flops | bytes accessed | tf_op | source)
XLA Modules:
  0.0 51.8 jit_solution(9229567870668429201)
XLA Ops:
  0.6 48.1 %shard_map.86 = (bf16[1,128,4096]{2,1,0:T(8,128)(2,1)}, bf16[512,512]{1,0:T(8,128)(2,1)}) custom-call(s32[1,8]{1,0:T(1,128)} %seg_ref.1, bf16[1,128,4096]{2,1,0:T(8,128)(2,1)} %hidden_ref.1, bf16[1,128,4096]{2,1,0:T(8,128)(2,1)} %query_ref.1, bf16[1,128,256]{2,1,0:T(8,128)(2,1)} %key_ref.1, bf16[1,128,256]{2,1,0:T(8,128)(2,1)} %value_ref.1, ...), custom_call_target="tpu_custom_call" | custom-call | tf_op jit(solution)/shard_map/pallas_call | solution.py:407
  48.7 0.0 copy-start
  48.7 2.3 %copy.11 = bf16[1,128,4096]{2,1,0:T(8,128)(2,1)} copy(bf16[1,128,4096]{2,1,0:T(8,128)(2,1)} %get-tuple-element.4) | data formatting | bytes 2097152
  51.1 0.0 copy-done
  51.1 0.8 %copy.12 = bf16[512,512]{1,0:T(8,128)(2,1)} copy(bf16[512,512]{1,0:T(8,128)(2,1)S(1)} %copy-done) | data formatting | bytes 1048576
Async XLA Ops:
  48.7 2.4 %copy-start = (bf16[512,512]{1,0:T(8,128)(2,1)S(1)}, bf16[512,512]{1,0:T(8,128)(2,1)}, u32[]{:S(2)}) copy-start(bf16[512,512]{1,0:T(8,128)(2,1)} %get-tuple-element.5) | copy-start | bytes 1572868
